TPU v7x, 512 devices: a whole 4x8x8 slice. The times are simulated.
512 devices in a mesh: rows: 128 (over z, y, core), rep: 4 (over x).
Axes of the slice: x: 4, y: 8, z: 8, core: 2. Of those that a mesh axis runs over, the one named last changes fastest.
Arguments:
- event_slots: int32 [512, 128], P(('rows', 'rep')), may hold values from 0 to 383, as said below
- fetch_rows: int32 [512, 256], P(('rows', 'rep')), may hold values from 0 to 255, as said below
- fetch_counts: int32 [512, 128], P(('rows', 'rep')), may hold values from 1 to 2, as said below
- hot_table: float32 [128, 512], replicated, may hold values from -6 to 6
- hot_accum: float32 [128], replicated, may hold values from 0.05 to 2
- cold_table: float32 [32768, 512], P('rows'), may hold values from -6 to 6
- cold_accum: float32 [32768], P('rows'), may hold values from 0.05 to 2
- ln_gain: float32 [512], replicated, may hold values from 0.1 to 1.9
- ln_bias: float32 [512], replicated, may hold values from -3 to 3
- w_in: bfloat16 [512, 2048], replicated, may hold values from -0.25 to 0.25
- w_out: bfloat16 [512, 512], replicated, may hold values from -0.25 to 0.25
- out_grad: bfloat16 [65536, 512], P(('rows', 'rep')), may hold values from -6 to 6
Outputs:
- new_hot_table: float32 [128, 512], replicated
- new_hot_accum: float32 [128], replicated
- new_cold_table: float32 [32768, 512], P('rows')
- new_cold_accum: float32 [32768], P('rows')
Inputs may be any that keep to these rules, and one draw needn't show every extreme that they name: `event_slots`: rows of the lookup buffer: the 128 hot rows, then 2 slots for each of the 128 owners; an event names slot k of owner j only if k is below that device's fetch_counts for j. `fetch_rows`: rows local to the owner's shard, distinct within one owner's 2 slots of one device; slots at or past the count are padding. `fetch_counts`: some owner is asked for 2 rows by every device.
All inputs are finite; a program needn't handle non-finite values.
Results may differ from a plain program's by a relative error of at most 0.0065.
Values sent between devices are 32-bit elements; how exact they have to be, the bound alone decides.
A program may use at most 64 MiB of HBM per device.

v0:
```python
import jax
import jax.numpy as jnp
from jax import lax
from jax.sharding import Mesh
from jax.sharding import PartitionSpec as P

HEAD = 128
ROWS = ("rows_0", "rows_1", "rows_2")
ROWS_REP = ("rows_0", "rows_1", "rows_2", "rep")


STEP_RATE = 0.5


def split_up(value, dim, peers):
    dims = value.shape
    parts = value.reshape(*dims[:dim], peers, dims[dim] // peers, *dims[dim + 1 :])
    return jnp.moveaxis(parts, dim, 0)


def summed_on_arrival(value, axis, dim):
    peers = lax.axis_size(axis)
    parts = lax.all_to_all(split_up(value, dim, peers), axis, 0, 0, tiled=True)
    return jnp.sum(parts, axis=0)


def summed_rows(value, axes, dim):
    far, near = axes
    own = summed_on_arrival(split_up(value, dim, lax.axis_size(far)), near, dim + 1)
    return jnp.sum(lax.all_to_all(own, far, 0, 0, tiled=True), axis=0)


def filled_up(lines, peers):
    spare = -lines.shape[0] % peers
    if not spare:
        return lines
    return jnp.concatenate([lines, jnp.zeros((spare, *lines.shape[1:]), lines.dtype)])


def from_everyone(value, axis):
    peers = lax.axis_size(axis)
    return lax.all_to_all(
        jnp.broadcast_to(value[None], (peers, *value.shape)), axis, 0, 0, tiled=True
    )


def in_order(parts, dim):
    dims = list(parts.shape[1:])
    dims[dim] *= parts.shape[0]
    return jnp.moveaxis(parts, 0, dim).reshape(dims)


def gather_axes(value, axes, dim):
    far, near = axes
    initial = from_everyone(value, far)
    parts = jnp.swapaxes(from_everyone(initial, near), 0, 1)
    return in_order(parts.reshape(-1, *value.shape), dim)


def nested_sum(value, axes):
    lines = value.reshape(-1)
    own = summed_rows(filled_up(lines, lax.axis_size(axes[0]) * lax.axis_size(axes[1])), axes, 0)
    whole = gather_axes(own, axes, 0)
    return whole[: len(lines)].reshape(value.shape)


def over_copies(value, axis):
    everything = from_everyone(value, axis)
    return jnp.sum(everything, axis=0)


def hstu_layer(looked_up, ln_gain, ln_bias, w_in, w_out):
    seq_rows = looked_up.shape[0]
    inner = w_out.shape[0]
    n_heads = inner // HEAD
    row_mean = jnp.mean(looked_up, axis=1, keepdims=True)
    centered = looked_up - row_mean
    row_var = jnp.mean(centered * centered, axis=1, keepdims=True)
    normed = (centered * lax.rsqrt(row_var + 1e-05) * ln_gain + ln_bias).astype(jnp.bfloat16)
    projected = jax.nn.silu(jnp.dot(normed, w_in, preferred_element_type=jnp.float32)).astype(
        jnp.bfloat16
    )
    gates_u, values_v, queries, keys_k = jnp.split(projected, 4, axis=1)
    head_shape = (seq_rows, n_heads, HEAD)
    scores = jnp.einsum(
        "qhd,khd->hqk",
        queries.reshape(head_shape),
        keys_k.reshape(head_shape),
        preferred_element_type=jnp.float32,
    ) * HEAD ** (-0.5)
    causal = (
        lax.broadcasted_iota(jnp.int32, (seq_rows, seq_rows), 0)
        >= lax.broadcasted_iota(jnp.int32, (seq_rows, seq_rows), 1)
    ).astype(jnp.float32)
    attention = (jax.nn.silu(scores) * causal * (1.0 / seq_rows)).astype(jnp.bfloat16)
    mixed_val = jnp.einsum(
        "hqk,khd->qhd", attention, values_v.reshape(head_shape), preferred_element_type=jnp.float32
    ).reshape(seq_rows, inner)
    mixed_mean = jnp.mean(mixed_val, axis=1, keepdims=True)
    mixed_cent = mixed_val - mixed_mean
    mixed_var = jnp.mean(mixed_cent * mixed_cent, axis=1, keepdims=True)
    gated_val = (mixed_cent * lax.rsqrt(mixed_var + 1e-06) * gates_u.astype(jnp.float32)).astype(
        jnp.bfloat16
    )
    layer_out = looked_up + jnp.dot(gated_val, w_out, preferred_element_type=jnp.float32)
    return layer_out.astype(jnp.bfloat16)


def adagrad(table_rows, accum_rows, grad_rows):
    new_accum = accum_rows + jnp.mean(grad_rows * grad_rows, axis=1)
    return (table_rows - STEP_RATE * grad_rows * lax.rsqrt(new_accum)[:, None], new_accum)


def on_device(
    event_slots,
    fetch_rows,
    fetch_counts,
    hot_table,
    hot_accum,
    cold_table,
    cold_accum,
    ln_gain,
    ln_bias,
    w_in,
    w_out,
    out_grad,
):
    owner_count = lax.axis_size(ROWS)
    per_owner = fetch_rows.shape[1] // owner_count
    hot_rows, feature_width = hot_table.shape
    rows_shard = cold_table.shape[0]
    wanted_rows = fetch_rows.reshape(owner_count, per_owner)
    live_mask = (
        lax.broadcasted_iota(jnp.int32, (owner_count, per_owner), 1)
        < fetch_counts.reshape(owner_count, 1)
    ).astype(jnp.float32)[:, :, None]
    asked_rows = lax.all_to_all(wanted_rows, ROWS, split_axis=0, concat_axis=0, tiled=True)
    found = cold_table[asked_rows]
    fetched = lax.all_to_all(found, ROWS, split_axis=0, concat_axis=0, tiled=True)
    buffer = jnp.concatenate(
        [hot_table, (fetched * live_mask).reshape(owner_count * per_owner, feature_width)], axis=0
    )
    event_rows = event_slots.reshape(-1)
    looked_up = buffer[event_rows]

    def forward(lookup_rows):
        return hstu_layer(lookup_rows, ln_gain, ln_bias, w_in, w_out)

    _, backward = jax.vjp(forward, looked_up)
    (d_lookup,) = backward(out_grad)
    buffer_grad = jax.ops.segment_sum(
        d_lookup, event_rows, num_segments=hot_rows + owner_count * per_owner
    )
    returned = buffer_grad[hot_rows:].reshape(owner_count, per_owner, feature_width) * live_mask
    arrived = lax.all_to_all(returned, ROWS, split_axis=0, concat_axis=0, tiled=True)
    cold_grad = jax.ops.segment_sum(
        arrived.reshape(-1, feature_width), asked_rows.reshape(-1), num_segments=rows_shard
    )
    hot_grad = buffer_grad[:hot_rows]
    summed_hot = nested_sum(hot_grad, (("rows_0", "rows_1"), ("rows_2", "rep")))
    new_hot_table, new_hot_accum = adagrad(hot_table, hot_accum, summed_hot)
    summed_cold = over_copies(cold_grad, "rep")
    new_cold_table, new_cold_accum = adagrad(cold_table, cold_accum, summed_cold)
    return (new_hot_table, new_hot_accum, new_cold_table, new_cold_accum)


def solution(mesh):
    finer = Mesh(
        mesh.devices.reshape(8, 8, 2, mesh.shape["rep"]), ("rows_0", "rows_1", "rows_2", "rep")
    )
    return jax.shard_map(
        on_device,
        mesh=finer,
        in_specs=(
            P(ROWS_REP, None),
            P(ROWS_REP, None),
            P(ROWS_REP, None),
            P(),
            P(),
            P(ROWS, None),
            P(ROWS),
            P(),
            P(),
            P(),
            P(),
            P(ROWS_REP, None),
        ),
        out_specs=(P(), P(), P(ROWS, None), P(ROWS)),
        check_vma=False,
    )
```

profile of v0, /device:TPU:1, one launch (start us, length us, event | category | flops | bytes accessed | tf_op | source)
XLA Modules:
  0.0 200.4 jit_solution(9803074104284010522)
XLA Ops:
  0.6 0.5 broadcast.188
  1.2 1.5 reduce.13
  2.6 0.1 all_to_all.33
  2.8 29.7 %all_to_all.52 = s32[128,1,2]{2,1,0:T(1,128)S(1)} all-to-all(s32[128,1,2]{2,1,0:T(1,128)S(1)} %bitcast.83), channel_id=1, replica_groups=mesh['rows_0'=8,'rows_1'=8,'rows_2'=2,'rep'=4] {'rows_0','rows_1','rows_2'}, dimensions={0} | all-to-all | bytes 2048 | tf_op jit(solution)/shard_map/all_to_all | solution.py:137
  32.4 0.1 reshape.217
  32.6 2.3 %gather_fusion = f32[256,512]{1,0:T(8,128)S(1)} fusion(f32[256,512]{1,0:T(8,128)} %param.17, s32[1024]{0:T(1024)S(1)} %pad_clamp_fusion.1), kind=kCustom, calls=%fused_computation | custom fusion | bytes 1049600 | tf_op jit(solution)/shard_map/gather | solution.py:138
  34.9 1.1 reshape.216
  36.0 5.8 %all-to-all-start.1 = ((f32[128,2,512]{2,1,0:T(2,128)}), f32[128,2,512]{2,1,0:T(2,128)S(1)}, u32[]{:S(2)}, u32[]{:S(2)}) async-start(f32[128,2,512]{2,1,0:T(2,128)} %reshape.216), calls=%async_computation.1 | async-start | bytes 1048576 | tf_op jit(solution)/shard_map/all_to_all | solution.py:139
  41.8 0.6 fusion.43
  42.4 0.6 fusion.42
  43.1 19.3 %all-to-all-done.1 = f32[128,2,512]{2,1,0:T(2,128)S(1)} async-done(((f32[128,2,512]{2,1,0:T(2,128)}), f32[128,2,512]{2,1,0:T(2,128)S(1)}, u32[]{:S(2)}, u32[]{:S(2)}) %all-to-all-start.1) | async-done | bytes 524320 | tf_op jit(solution)/shard_map/all_to_all | solution.py:139
  62.4 1.1 broadcast_multiply_fusion.1
  63.5 1.4 reshape.204
  64.9 1.0 pad_maximum_fusion
  65.9 0.8 gather_fusion.1
  66.8 0.2 multiply_reduce_fusion.4
  67.0 1.5 multiply_convert_fusion
  68.6 0.8 copy-done.3
  69.4 0.1 copy.108
  69.5 0.1 copy.107
  69.6 0.2 convolution_multiply_fusion
  69.9 1.2 fusion.52
  71.2 0.1 copy.101
  71.4 1.5 multiply_reduce_fusion.3
  72.9 1.7 fusion.51
  74.6 0.3 convolution_convert_fusion.3
  75.0 0.3 fusion.21
  75.3 0.2 fusion.53
  75.5 0.2 fusion.54
  75.7 0.1 copy.104
  75.8 0.1 copy.105
  75.9 0.1 copy.106
  76.1 2.2 %multiply_reduce_fusion.2 = (f32[128]{0:T(128)S(1)}, f32[128,512]{1,0:T(8,128)S(1)}) fusion(f32[128,512]{1,0:T(8,128)S(1)} %gather_fusion.1, f32[128]{0:T(128)S(1)} %broadcast_multiply_fusion.3, f32[512]{0:T(512)S(1)} %copy-done.19, bf16[512,2048]{1,0:T(8,128)(2,1)S(1)} %copy-done, f32[128,2048]{1,0:T(8,128)} %get-tuple-element.19, ...), kind=kOutput, calls=%fused_computation.52 | convolution fusion | flops 273284992 | bytes 4197376 | tf_op jit(solution)/shard_map/transpose(jvp())/dot_general | solution.py:80
  78.3 0.2 fusion.50
  78.5 2.0 scatter_custom_fusion
  80.6 10.8 %all_to_all.53 = f32[8,64,128]{2,1,0:T(8,128)S(1)} all-to-all(f32[8,64,128]{2,1,0:T(8,128)S(1)} %copy.97), channel_id=1, replica_groups=mesh['rows_0'=8,'rows_1'=8,'rows_2'=2,'rep'=4] {'rows_2','rep'}, dimensions={0} | all-to-all | bytes 524288 | tf_op jit(solution)/shard_map/all_to_all | solution.py:23
  91.4 0.6 reduce_sum.148
  92.0 5.6 %all-to-all-start.3 = ((f32[64,1,128]{2,1,0:T(1,128)}), f32[64,1,128]{2,1,0:T(1,128)}, u32[]{:S(2)}, u32[]{:S(2)}) async-start(f32[64,1,128]{2,1,0:T(1,128)} %bitcast.18), calls=%async_computation.3 | async-start | bytes 65536 | tf_op jit(solution)/shard_map/all_to_all | solution.py:30
  97.7 0.3 reshape.213
  98.0 10.2 %all-to-all-done.3 = f32[64,1,128]{2,1,0:T(1,128)} async-done(((f32[64,1,128]{2,1,0:T(1,128)}), f32[64,1,128]{2,1,0:T(1,128)}, u32[]{:S(2)}, u32[]{:S(2)}) %all-to-all-start.3) | async-done | bytes 32800 | tf_op jit(solution)/shard_map/all_to_all | solution.py:30
  108.2 0.8 reduce_sum.149
  109.0 0.6 broadcast_in_dim.25
  109.7 5.4 %all-to-all-start.4 = ((f32[64,1,128]{2,1,0:T(1,128)}), f32[64,1,128]{2,1,0:T(1,128)}, u32[]{:S(2)}, u32[]{:S(2)}) async-start(f32[64,1,128]{2,1,0:T(1,128)} %broadcast_in_dim.25), calls=%async_computation.4 | async-start | bytes 65536 | tf_op jit(solution)/shard_map/all_to_all | solution.py:42
  115.1 0.3 broadcast_multiply_fusion
  115.4 10.4 %all-to-all-done.4 = f32[64,1,128]{2,1,0:T(1,128)} async-done(((f32[64,1,128]{2,1,0:T(1,128)}), f32[64,1,128]{2,1,0:T(1,128)}, u32[]{:S(2)}, u32[]{:S(2)}) %all-to-all-start.4) | async-done | bytes 32800 | tf_op jit(solution)/shard_map/all_to_all | solution.py:42
  125.8 27.6 %all_to_all.54 = f32[128,2,512]{2,1,0:T(2,128)S(1)} all-to-all(f32[128,2,512]{2,1,0:T(2,128)S(1)} %broadcast_multiply_fusion), channel_id=1, replica_groups=mesh['rows_0'=8,'rows_1'=8,'rows_2'=2,'rep'=4] {'rows_0','rows_1','rows_2'}, dimensions={0} | all-to-all | bytes 1048576 | tf_op jit(solution)/shard_map/all_to_all | solution.py:155
  153.4 1.5 broadcast_in_dim.27
  154.8 3.4 %all-to-all-start.5 = ((f32[8,64,128]{2,1,0:T(8,128)}), f32[8,64,128]{2,1,0:T(8,128)S(1)}, u32[]{:S(2)}, u32[]{:S(2)}) async-start(f32[8,64,128]{2,1,0:T(8,128)} %broadcast_in_dim.27), calls=%async_computation.5 | async-start | bytes 524288 | tf_op jit(solution)/shard_map/all_to_all | solution.py:42
  158.2 0.8 reduce.14
  159.0 0.1 reshape.241
  159.2 0.4 reshape.243
  159.5 2.2 %scatter_custom_fusion.1 = f32[256,512]{1,0:T(8,128)S(1)} fusion(s32[256]{0:T(256)S(1)} %reshape.241, f32[256,512]{1,0:T(8,128)S(1)} %reshape.243, f32[]{:T(128)} %constant.13.clone.1), kind=kCustom, calls=%fused_computation.46 | custom fusion | flops 131072 | bytes 524292 | tf_op jit(solution)/shard_map/scatter-add | solution.py:156
  161.8 2.8 %all-to-all-done.5 = f32[8,64,128]{2,1,0:T(8,128)S(1)} async-done(((f32[8,64,128]{2,1,0:T(8,128)}), f32[8,64,128]{2,1,0:T(8,128)S(1)}, u32[]{:S(2)}, u32[]{:S(2)}) %all-to-all-start.5) | async-done | bytes 262176 | tf_op jit(solution)/shard_map/all_to_all | solution.py:42
  164.6 1.6 broadcast_in_dim.29
  166.1 4.6 %all-to-all-start.7 = ((f32[4,256,512]{2,1,0:T(8,128)}), f32[4,256,512]{2,1,0:T(8,128)}, u32[]{:S(2)}, u32[]{:S(2)}) async-start(f32[4,256,512]{2,1,0:T(8,128)} %broadcast_in_dim.29), calls=%async_computation.7 | async-start | bytes 4194304 | tf_op jit(solution)/shard_map/all_to_all | solution.py:42
  170.7 0.1 multiply_reduce_fusion.1
  171.1 0.2 copy.98
  171.4 0.5 rsqrt_multiply_fusion.1
  171.9 0.8 multiply_subtract_fusion.1
  172.7 24.2 %all-to-all-done.7 = f32[4,256,512]{2,1,0:T(8,128)} async-done(((f32[4,256,512]{2,1,0:T(8,128)}), f32[4,256,512]{2,1,0:T(8,128)}, u32[]{:S(2)}, u32[]{:S(2)}) %all-to-all-start.7) | async-done | bytes 2097184 | tf_op jit(solution)/shard_map/all_to_all | solution.py:42
  196.9 1.9 reduce_sum.153
  198.7 0.1 multiply_reduce_fusion
  198.9 0.6 rsqrt_multiply_fusion
  199.4 0.9 multiply_subtract_fusion
  (64 shorter events, 0.9 us)
Async XLA Ops:
  0.6 66.4 %copy-start = (bf16[512,2048]{1,0:T(8,128)(2,1)S(1)}, bf16[512,2048]{1,0:T(8,128)(2,1)}, u32[]{:S(2)}) copy-start(bf16[512,2048]{1,0:T(8,128)(2,1)} %param.21) | copy-start | bytes 6291460
  34.9 6.9 %copy-start.20 = (s32[1,128]{1,0:T(1,128)S(1)}, s32[1,128]{1,0:T(1,128)}, u32[]{:S(2)}) copy-start(s32[1,128]{1,0:T(1,128)} %param.12) | copy-start | bytes 1540
  34.9 8.2 %copy-start.13 = (s32[1,128]{1,0:T(1,128)S(1)}, s32[1,128]{1,0:T(1,128)}, u32[]{:S(2)}) copy-start(s32[1,128]{1,0:T(1,128)} %param.14) | copy-start | bytes 1540
  36.0 26.5 %all-to-all-start.1 = ((f32[128,2,512]{2,1,0:T(2,128)}), f32[128,2,512]{2,1,0:T(2,128)S(1)}, u32[]{:S(2)}, u32[]{:S(2)}) async-start(f32[128,2,512]{2,1,0:T(2,128)} %reshape.216), calls=%async_computation.1 | async-start | bytes 1048576 | tf_op jit(solution)/shard_map/all_to_all | solution.py:139
  64.9 2.1 %copy-start.17 = (f32[512]{0:T(512)S(1)}, f32[512]{0:T(512)}, u32[]{:S(2)}) copy-start(f32[512]{0:T(512)} %param.20) | copy-start | bytes 6148
  65.9 1.1 copy-start.18
  67.0 1.6 copy-start.14
  68.6 0.8 copy-start.3
  68.6 2.7 %copy-start.4 = (bf16[128,512]{1,0:T(8,128)(2,1)S(1)}, bf16[128,512]{1,0:T(8,128)(2,1)}, u32[]{:S(2)}) copy-start(bf16[128,512]{1,0:T(8,128)(2,1)} %param.23) | copy-start | bytes 393220
  69.4 3.5 %copy-start.7 = (bf16[16,4,8,128]{3,2,1,0:T(8,128)(2,1)}, bf16[16,4,8,128]{3,2,1,0:T(8,128)(2,1)S(1)}, u32[]{:S(2)}) copy-start(bf16[16,4,8,128]{3,2,1,0:T(8,128)(2,1)S(1)} %get-tuple-element.13) | copy-start | bytes 393220
  69.9 1.3 copy-start.5
  71.3 3.3 %copy-start.6 = (f32[4,128,128]{2,1,0:T(8,128)S(1)}, f32[4,128,128]{2,1,0:T(8,128)}, u32[]{:S(2)}) copy-start(f32[4,128,128]{2,1,0:T(8,128)} %copy-done.5) | copy-start | bytes 786436
  71.3 3.3 %copy-start.11 = (f32[128,128]{1,0:T(8,128)S(1)}, f32[128,128]{1,0:T(8,128)}, u32[]{:S(2)}) copy-start(f32[128,128]{1,0:T(8,128)} %fusion.43) | copy-start | bytes 196612
  71.4 3.6 %copy-start.10 = (f32[128,128]{1,0:T(8,128)S(1)}, f32[128,128]{1,0:T(8,128)}, u32[]{:S(2)}) copy-start(f32[128,128]{1,0:T(8,128)} %fusion.42) | copy-start | bytes 196612
  72.9 2.1 %copy-start.8 = (bf16[16,4,8,128]{3,2,1,0:T(8,128)(2,1)S(1)}, bf16[16,4,8,128]{3,2,1,0:T(8,128)(2,1)}, u32[]{:S(2)}) copy-start(bf16[16,4,8,128]{3,2,1,0:T(8,128)(2,1)} %copy-done.7) | copy-start | bytes 393220
  75.0 1.1 copy-start.9
  75.0 1.1 copy-start.19
  76.1 2.2 %copy-start.15 = (f32[128]{0:T(128)S(1)}, f32[128]{0:T(128)}, u32[]{:S(2)}) copy-start(f32[128]{0:T(128)} %copy-done.14) | copy-start | bytes 1540
  92.0 16.2 %all-to-all-start.3 = ((f32[64,1,128]{2,1,0:T(1,128)}), f32[64,1,128]{2,1,0:T(1,128)}, u32[]{:S(2)}, u32[]{:S(2)}) async-start(f32[64,1,128]{2,1,0:T(1,128)} %bitcast.18), calls=%async_computation.3 | async-start | bytes 65536 | tf_op jit(solution)/shard_map/all_to_all | solution.py:30
  109.7 16.1 %all-to-all-start.4 = ((f32[64,1,128]{2,1,0:T(1,128)}), f32[64,1,128]{2,1,0:T(1,128)}, u32[]{:S(2)}, u32[]{:S(2)}) async-start(f32[64,1,128]{2,1,0:T(1,128)} %broadcast_in_dim.25), calls=%async_computation.4 | async-start | bytes 65536 | tf_op jit(solution)/shard_map/all_to_all | solution.py:42
  154.8 9.7 %all-to-all-start.5 = ((f32[8,64,128]{2,1,0:T(8,128)}), f32[8,64,128]{2,1,0:T(8,128)S(1)}, u32[]{:S(2)}, u32[]{:S(2)}) async-start(f32[8,64,128]{2,1,0:T(8,128)} %broadcast_in_dim.27), calls=%async_computation.5 | async-start | bytes 524288 | tf_op jit(solution)/shard_map/all_to_all | solution.py:42
  166.1 5.2 %copy-start.16 = (f32[128]{0:T(128)S(1)}, f32[128]{0:T(128)}, u32[]{:S(2)}) copy-start(f32[128]{0:T(128)} %param.16) | copy-start | bytes 1540
  166.1 5.8 %copy-start.2 = (f32[128,512]{1,0:T(8,128)S(1)}, f32[128,512]{1,0:T(8,128)}, u32[]{:S(2)}) copy-start(f32[128,512]{1,0:T(8,128)} %param.15) | copy-start | bytes 786436
  166.1 30.7 %all-to-all-start.7 = ((f32[4,256,512]{2,1,0:T(8,128)}), f32[4,256,512]{2,1,0:T(8,128)}, u32[]{:S(2)}, u32[]{:S(2)}) async-start(f32[4,256,512]{2,1,0:T(8,128)} %broadcast_in_dim.29), calls=%async_computation.7 | async-start | bytes 4194304 | tf_op jit(solution)/shard_map/all_to_all | solution.py:42
  171.4 27.5 %copy-start.12 = (f32[256]{0:T(256)S(1)}, f32[256]{0:T(256)}, u32[]{:S(2)}) copy-start(f32[256]{0:T(256)} %param.18) | copy-start | bytes 3076
  171.4 28.1 %copy-start.1 = (f32[256,512]{1,0:T(8,128)S(1)}, f32[256,512]{1,0:T(8,128)}, u32[]{:S(2)}) copy-start(f32[256,512]{1,0:T(8,128)} %param.17) | copy-start | bytes 1572868
where the time goes:
time: 201 us; the launch traced here: 200 us
  blocking collectives  68 us (34%)
  waiting for transfers between devices  66.9 us (33%)
  starting transfers between devices  24.8 us (12%)
  other arithmetic  19 us (9%)
  local copies, waits for them, and re-layouts  12.9 us (6%)
  matrix products  7.64 us (4%)
    all_to_all x3, waiting for transfers between devices, from_everyone(): lax.all_to_all(jnp.broadcast_to(value[None], (peers, *value.shape)), axis...  37.4 us
    all_to_all x1, blocking collectives, on_device(): lax.all_to_all(wanted_rows, ROWS, split_axis=0, concat_axis=0, tiled=True)  29.7 us
    all_to_all x1, blocking collectives, on_device(): lax.all_to_all(returned, ROWS, split_axis=0, concat_axis=0, tiled=True)  27.6 us
    all_to_all x1, waiting for transfers between devices, on_device(): lax.all_to_all(found, ROWS, split_axis=0, concat_axis=0, tiled=True)  19.3 us
    all_to_all x3, starting transfers between devices, from_everyone(): lax.all_to_all(jnp.broadcast_to(value[None], (peers, *value.shape)), axis...  13.4 us
    all_to_all x1, blocking collectives, summed_on_arrival(): parts = lax.all_to_all(split_up(value, dim, peers), axis, 0, 0, tiled=True)  10.8 us
    all_to_all x1, waiting for transfers between devices, summed_rows(): return jnp.sum(lax.all_to_all(own, far, 0, 0, tiled=True), axis=0)  10.2 us
    all_to_all x1, starting transfers between devices, on_device(): lax.all_to_all(found, ROWS, split_axis=0, concat_axis=0, tiled=True)  5.76 us
  transfers between devices with their start and end apart: 5, of which 5 were waited for; matrix products, arithmetic and copies ran while one was open for 4% of the time, Pallas kernels for 0%

commit v1 on v0

v1 whole, which is shorter than its diff:
```python
import functools

import jax
import jax.numpy as jnp
from jax import lax
from jax.experimental import pallas as pl
from jax.experimental.pallas import tpu as pltpu
from jax.sharding import Mesh
from jax.sharding import PartitionSpec as P

HEAD = 128
STEP_RATE = 0.5
NZ, NY, NC, NX = 8, 8, 2, 4
NYC = NY * NC
OWNERS = NZ * NYC
ALL = ("z", "y", "c", "x")
BY_ROWS = ("z", "y", "c")
MESH = pl.DeviceIdType.MESH
F32, BF16 = jnp.float32, jnp.bfloat16


def dot(a, b, dims=((1,), (0,))):
    return lax.dot_general(a, b, (dims, ((), ())), preferred_element_type=F32)


def two_parts(value):
    high = value.astype(BF16)
    low = (value - high.astype(F32)).astype(BF16)
    return high, low


def picked(onehot, value, dims=((1,), (0,))):
    high, low = two_parts(value)
    return dot(onehot, high, dims) + dot(onehot, low, dims)


def sigmoid(x):
    return 0.5 * jnp.tanh(0.5 * x) + 0.5


def iota(shape, dim):
    return lax.broadcasted_iota(jnp.int32, shape, dim)


def layer_gradient(looked_up, gain, bias, w_in_ref, w_out_ref, out_grad):
    seq, width = looked_up.shape
    inner = w_out_ref.shape[0]
    mean = jnp.mean(looked_up, axis=1, keepdims=True)
    centered = looked_up - mean
    inv = lax.rsqrt(jnp.mean(centered * centered, axis=1, keepdims=True) + 1e-05)
    xhat = centered * inv
    normed = (xhat * gain + bias).astype(BF16)
    parts, slopes = [], []
    for b in range(4):
        pre = dot(normed, w_in_ref[:, b * inner : (b + 1) * inner])
        sig = sigmoid(pre)
        act = pre * sig
        parts.append(act.astype(BF16))
        slopes.append(sig + act * (1.0 - sig))
    gates, values, queries, keys = parts
    causal = iota((seq, seq), 0) >= iota((seq, seq), 1)
    scale = HEAD ** (-0.5)
    heads = [slice(h * HEAD, (h + 1) * HEAD) for h in range(inner // HEAD)]
    attention, slope_att, mixed = [], [], []
    for h in heads:
        scores = dot(queries[:, h], keys[:, h], ((1,), (1,))) * scale
        sig = sigmoid(scores)
        act = scores * sig
        att = jnp.where(causal, act * (1.0 / seq), 0.0).astype(BF16)
        attention.append(att)
        slope_att.append(jnp.where(causal, (sig + act * (1.0 - sig)) * (scale / seq), 0.0))
        mixed.append(dot(att, values[:, h]))
    mixed = jnp.concatenate(mixed, axis=1)
    mixed = mixed - jnp.mean(mixed, axis=1, keepdims=True)
    inv2 = lax.rsqrt(jnp.mean(mixed * mixed, axis=1, keepdims=True) + 1e-06)
    mhat = mixed * inv2
    d_gated = dot(out_grad, w_out_ref[...], ((1,), (1,))).astype(BF16).astype(F32)
    d_gates = (d_gated * mhat).astype(BF16)
    d_mhat = d_gated * gates.astype(F32)
    d_mixed = inv2 * (
        d_mhat
        - jnp.mean(d_mhat, axis=1, keepdims=True)
        - mhat * jnp.mean(d_mhat * mhat, axis=1, keepdims=True)
    )
    d_mixed = d_mixed.astype(BF16)
    d_values, d_queries, d_keys = [], [], []
    for n, h in enumerate(heads):
        d_att = dot(d_mixed[:, h], values[:, h], ((1,), (1,))).astype(BF16).astype(F32)
        d_values.append(dot(attention[n], d_mixed[:, h], ((0,), (0,))).astype(BF16))
        d_raw = (d_att * slope_att[n]).astype(BF16)
        d_queries.append(dot(d_raw, keys[:, h]).astype(BF16))
        d_keys.append(dot(d_raw, queries[:, h], ((0,), (0,))).astype(BF16))
    d_parts = [
        d_gates,
        jnp.concatenate(d_values, axis=1),
        jnp.concatenate(d_queries, axis=1),
        jnp.concatenate(d_keys, axis=1),
    ]
    d_normed = jnp.zeros((seq, width), F32)
    for b in range(4):
        d_pre = (d_parts[b].astype(F32) * slopes[b]).astype(BF16)
        d_normed = d_normed + dot(d_pre, w_in_ref[:, b * inner : (b + 1) * inner], ((1,), (1,)))
    d_xhat = d_normed.astype(BF16).astype(F32) * gain
    return out_grad.astype(F32) + inv * (
        d_xhat
        - jnp.mean(d_xhat, axis=1, keepdims=True)
        - xhat * jnp.mean(d_xhat * xhat, axis=1, keepdims=True)
    )


def step_kernel(
    slots_ref,
    rows_ref,
    counts_ref,
    hot_ref,
    table_ref,
    gain_ref,
    bias_ref,
    w_in_ref,
    w_out_ref,
    out_grad_ref,
    cold_out,
    hot_out,
    idx_z,
    idx_n,
    idx_all,
    idx_x,
    send_a,
    recv_a,
    x_send,
    x_recv,
    send_b,
    recv_b,
    hot_c,
    hot_cr,
    hot_z,
    hot_zr,
    hot_t,
    hot_yr,
    hot_g,
    hot_f,
    sems,
    z_s,
    z_r,
    yc_s,
    yc_r,
    xi_s,
    xi_r,
    xh_s,
    xh_r,
    xc_s,
    xc_r,
    hz_s,
    hz_r,
    hy_s,
    hy_r,
    hg_s,
    hg_r,
    xo_s,
    xo_r,
    xp_s,
    xp_r,
):
    z, y, c, x = (lax.axis_index(a) for a in ALL)
    yc = y * NC + c
    me = yc * NZ + z
    width = hot_ref.shape[1]
    lanes = width // NX

    def along(axis, o):
        if axis == "z":
            t = lax.rem(z + o, NZ)
            return t, (t, y, c, x)
        if axis == "y":
            t = lax.rem(y + o, NY)
            return t, (z, t, c, x)
        if axis == "yc":
            t = lax.rem(yc + o, NYC)
            return t, (z, lax.div(t, NC), lax.rem(t, NC), x)
        t = lax.rem(x + o, NX)
        return t, (z, y, c, t)

    SIZE = {"z": NZ, "y": NY, "yc": NYC, "x": NX}

    def exchange(axis, src, dst, s, r):
        copies = []
        for o in range(1, SIZE[axis]):
            t, dev = along(axis, o)
            copies.append(
                pltpu.make_async_remote_copy(
                    src_ref=src(t),
                    dst_ref=dst,
                    send_sem=s.at[o],
                    recv_sem=r.at[o],
                    device_id=dev,
                    device_id_type=MESH,
                )
            )
        for cp in copies:
            cp.start()
        return copies

    def to_sibling(src, dst, n):
        cp = pltpu.make_async_remote_copy(
            src_ref=src,
            dst_ref=dst,
            send_sem=sems.at[n],
            recv_sem=sems.at[n + 1],
            device_id=(z, y, 1 - c, x),
            device_id_type=MESH,
        )
        cp.start()
        return cp

    def arrived(copies):
        for cp in copies:
            cp.wait_recv()

    def tile(q):
        return pl.ds(pl.multiple_of(q * 8, 8), 8)

    def scatter_tiles(src, dst, n):
        @pl.loop(1, OWNERS)
        def _(o):
            p = lax.rem(o * 37, OWNERS)
            tz = lax.rem(z + lax.rem(p, NZ), NZ)
            ty = lax.rem(y + lax.rem(lax.div(p, NZ), NY), NY)
            tc = lax.rem(c + lax.div(p, NZ * NY), NC)
            q = (ty * NC + tc) * NZ + tz
            pltpu.make_async_remote_copy(
                src_ref=src.at[tile(q)],
                dst_ref=dst.at[tile(me)],
                send_sem=sems.at[n],
                recv_sem=sems.at[n + 1],
                device_id=(tz, ty, tc, x),
                device_id_type=MESH,
            ).start()

    def tiles_wait(ref, n):
        whole = ref.at[pl.ds(0, (OWNERS - 1) * 8)]
        pltpu.make_async_copy(whole, whole, sems.at[n]).wait()

    barrier = pltpu.get_barrier_semaphore()
    greeted = 0
    for axis in ("z", "yc", "x"):
        for o in range(1, SIZE[axis]):
            pl.semaphore_signal(barrier, inc=1, device_id=along(axis, o)[1], device_id_type=MESH)
            greeted += 1
    pl.semaphore_wait(barrier, greeted)

    pending = exchange("z", lambda t: rows_ref, idx_z.at[z], z_s, z_r)
    idx_z[z] = rows_ref[...]
    table_high, table_low = two_parts(table_ref[...])
    arrived(pending)
    every = jnp.concatenate([idx_z[i] for i in range(NZ)], axis=0).astype(F32)
    mine = pltpu.roll(every, lax.rem(8 * 32 - 32 * z, 256), axis=1)[:, :128]
    idx_n[...] = mine
    more = exchange("yc", lambda t: idx_n, idx_all.at[yc], yc_s, yc_r)
    idx_all[yc] = mine
    pending += more
    arrived(more)
    asked = idx_all[...].reshape(OWNERS, 128)
    lane = iota((OWNERS, 128), 1)
    line = iota((OWNERS, table_ref.shape[0]), 1).astype(F32)
    columns = []
    for k in range(2):
        column = jnp.sum(jnp.where(lane == 2 * yc + k, asked, 0.0), axis=1, keepdims=True)
        columns.append(column)
        onehot = (column == line).astype(BF16)
        found = dot(onehot, table_high) + dot(onehot, table_low)
        for i in range(NX):
            send_a[pl.ds(k * NX + i, OWNERS, stride=8), :] = found[:, i * lanes : (i + 1) * lanes]
    scatter_tiles(send_a, recv_a, 0)
    recv_a[tile(me), :] = send_a[tile(me), :]

    both = jnp.where(lane == 0, columns[0], jnp.where(lane == 1, columns[1], 0.0))
    idx_n2 = jnp.transpose(both)[:8, :]
    idx_x[x] = idx_n2
    more = exchange("x", lambda t: idx_x.at[x], idx_x.at[x], xi_s, xi_r)
    pending += more

    owner_of = lambda q: lax.rem(q, NZ) * NYC + lax.div(q, NZ)
    slot_of = jnp.transpose(jnp.broadcast_to(slots_ref[...].astype(F32), (128, 128)))
    lane1 = iota((128, 128), 1)
    order = (iota((128, 128), 0) == owner_of(lane1)).astype(BF16)
    live = dot(jnp.broadcast_to(counts_ref[...].astype(F32), (8, 128)).astype(BF16), order)[:1, :]
    hot_rows = hot_ref.shape[0]
    pick_hot = (slot_of == lane1.astype(F32)).astype(BF16)
    picks = []
    for k in range(2):
        name = (hot_rows + 2 * owner_of(lane1) + k).astype(F32)
        picks.append(((slot_of == name) & (live > k)).astype(BF16))
    looked_hot = picked(pick_hot, hot_ref[...])

    tiles_wait(recv_a, 1)
    looked = []
    for i in range(NX):
        part = looked_hot[:, i * lanes : (i + 1) * lanes]
        for k in range(2):
            part = part + picked(picks[k], recv_a[pl.ds(k * NX + i, OWNERS, stride=8), :])
        looked.append(part)
    looked_up = jnp.concatenate(looked, axis=1)

    d_lookup = layer_gradient(
        looked_up, gain_ref[...], bias_ref[...], w_in_ref, w_out_ref, out_grad_ref[...]
    )

    high, low = two_parts(d_lookup)
    for b, pick in enumerate([pick_hot] + picks):
        total = dot(pick, high, ((0,), (0,))) + dot(pick, low, ((0,), (0,)))
        for i in range(NX):
            x_send[i, b * 128 : (b + 1) * 128, :] = total[:, i * lanes : (i + 1) * lanes]
    hot_part, cold_part = pl.ds(0, 128), pl.ds(128, 256)
    hot_x = exchange("x", lambda t: x_send.at[t, hot_part], x_recv.at[x, hot_part], xh_s, xh_r)
    cold_x = exchange("x", lambda t: x_send.at[t, cold_part], x_recv.at[x, cold_part], xc_s, xc_r)
    pending += hot_x + cold_x
    x_recv[x] = x_send[x]

    arrived(hot_x)
    hot = x_recv[0, :128] + x_recv[1, :128] + x_recv[2, :128] + x_recv[3, :128]
    hot_c[...] = hot.reshape(2, 64, 128)
    swap = to_sibling(hot_c.at[1 - c], hot_cr, 4)
    arrived(cold_x)
    for p in range(NX):
        for k in range(2):
            send_b[pl.ds(p * 2 + k, OWNERS, stride=8), :] = x_recv[
                p, 128 + k * 128 : 256 + k * 128, :
            ]
    swap.wait()
    hot_z[...] = (hot_c[c] + hot_cr[...]).reshape(NZ, 8, 128)
    hot_zs = exchange("z", lambda t: hot_z.at[t], hot_zr.at[z], hz_s, hz_r)
    hot_zr[z] = hot_z[z]
    pending += hot_zs
    scatter_tiles(send_b, recv_b, 2)
    recv_b[tile(me), :] = send_b[tile(me), :]
    arrived(hot_zs)
    hot_t[0] = jnp.sum(hot_zr[...], axis=0)
    hot_ys = exchange("y", lambda t: hot_t.at[0], hot_yr.at[y], hy_s, hy_r)
    hot_yr[y] = hot_t[0]
    pending += hot_ys
    arrived(hot_ys)
    hot_t[1] = jnp.sum(hot_yr[...], axis=0)
    hot_gs = exchange("z", lambda t: hot_t.at[1], hot_g.at[z], hg_s, hg_r)
    hot_g[z] = hot_t[1]
    pending += hot_gs
    arrived(hot_gs)
    hot_f[c] = hot_g[...].reshape(64, 128)
    swap = to_sibling(hot_f.at[c], hot_f.at[c], 6)
    swap.wait()
    hot_out[x] = hot_f[...].reshape(128, 128)
    hot_os = exchange("x", lambda t: hot_out.at[x], hot_out.at[x], xo_s, xo_r)
    pending += hot_os

    arrived(pending[2 * 0 + (NZ - 1) + (NYC - 1) : (NZ - 1) + (NYC - 1) + (NX - 1)])
    tall = iota((table_ref.shape[0], OWNERS), 0).astype(F32)
    sums = [
        (tall == idx_x[p, k : k + 1, :]).astype(BF16) for p in range(NX) for k in range(2)
    ]
    tiles_wait(recv_b, 3)
    grad = jnp.zeros((table_ref.shape[0], 128), F32)
    for n in range(8):
        grad = grad + picked(sums[n], recv_b[pl.ds(n, OWNERS, stride=8), :])
    cold_out[x] = grad
    cold_os = exchange("x", lambda t: cold_out.at[x], cold_out.at[x], xp_s, xp_r)
    pending += cold_os
    arrived(hot_os)
    arrived(cold_os)
    for cp in pending:
        cp.wait_send()
    tiles_wait(recv_a, 0)
    tiles_wait(recv_b, 2)


def step(slots, rows, counts, hot_table, cold_table, gain, bias, w_in, w_out, out_grad):
    vm = pl.BlockSpec(memory_space=pltpu.VMEM)
    dma = pltpu.SemaphoreType.DMA
    cold_rows, width = cold_table.shape
    f32 = lambda *s: pltpu.VMEM(s, F32)
    two = lambda n: [dma((n,)), dma((n,))]
    return pl.pallas_call(
        step_kernel,
        out_shape=(
            jax.ShapeDtypeStruct((NX, cold_rows, width // NX), F32),
            jax.ShapeDtypeStruct((NX, hot_table.shape[0], width // NX), F32),
        ),
        in_specs=[vm] * 10,
        out_specs=(vm, vm),
        scratch_shapes=[
            pltpu.VMEM((NZ, 1, 256), jnp.int32),
            f32(8, 128),
            f32(NYC, 8, 128),
            f32(NX, 8, 128),
            f32(OWNERS * 8, 128),
            f32(OWNERS * 8, 128),
            f32(NX, 384, 128),
            f32(NX, 384, 128),
            f32(OWNERS * 8, 128),
            f32(OWNERS * 8, 128),
            f32(2, 64, 128),
            f32(64, 128),
            f32(NZ, 8, 128),
            f32(NZ, 8, 128),
            f32(2, 8, 128),
            f32(NY, 8, 128),
            f32(NZ, 8, 128),
            f32(2, 64, 128),
            dma((8,)),
            *two(NZ),
            *two(NYC),
            *two(NX),
            *two(NX),
            *two(NX),
            *two(NZ),
            *two(NY),
            *two(NZ),
            *two(NX),
            *two(NX),
        ],
        compiler_params=pltpu.CompilerParams(
            collective_id=0, has_side_effects=True, vmem_limit_bytes=48 << 20
        ),
        cost_estimate=pl.CostEstimate(
            flops=1_500_000_000, bytes_accessed=6_000_000, transcendentals=400_000
        ),
        name="step",
    )(slots, rows, counts, hot_table, cold_table, gain, bias, w_in, w_out, out_grad)


def update(grad_ref, table_ref, accum_ref, new_table, new_accum):
    rows = table_ref.shape[0]
    lanes = grad_ref.shape[2]
    total = sum(grad_ref[i] * grad_ref[i] for i in range(NX))
    mean = jnp.sum(total, axis=1, keepdims=True) * (1.0 / table_ref.shape[1])
    for b in range(rows // 128):
        at = slice(b * 128, (b + 1) * 128)
        old = jnp.transpose(jnp.broadcast_to(accum_ref[:, at], (128, 128)))
        new = old + mean[at, :]
        new_accum[:, at] = jnp.transpose(new)[:1, :]
        rate = STEP_RATE * lax.rsqrt(new)
        for i in range(NX):
            col = slice(i * lanes, (i + 1) * lanes)
            new_table[at, col] = table_ref[at, col] - grad_ref[i, at, :] * rate


def adagrad_kernel(
    cold_ref, hot_ref, cold_table, cold_accum, hot_table, hot_accum, o_hot, o_hacc, o_cold, o_cacc
):
    update(hot_ref, hot_table, hot_accum, o_hot, o_hacc)
    update(cold_ref, cold_table, cold_accum, o_cold, o_cacc)


def adagrad(cold_grad, hot_grad, cold_table, cold_accum, hot_table, hot_accum):
    vm = pl.BlockSpec(memory_space=pltpu.VMEM)
    cold_accum, hot_accum = cold_accum.reshape(1, -1), hot_accum.reshape(1, -1)
    out = pl.pallas_call(
        adagrad_kernel,
        out_shape=tuple(
            jax.ShapeDtypeStruct(a.shape, F32)
            for a in (hot_table, hot_accum, cold_table, cold_accum)
        ),
        in_specs=[vm] * 6,
        out_specs=(vm,) * 4,
        compiler_params=pltpu.CompilerParams(vmem_limit_bytes=16 << 20),
        name="adagrad",
    )(cold_grad, hot_grad, cold_table, cold_accum, hot_table, hot_accum)
    return out[0], out[1].reshape(-1), out[2], out[3].reshape(-1)


def on_device(
    event_slots,
    fetch_rows,
    fetch_counts,
    hot_table,
    hot_accum,
    cold_table,
    cold_accum,
    ln_gain,
    ln_bias,
    w_in,
    w_out,
    out_grad,
):
    cold_grad, hot_grad = step(
        event_slots,
        fetch_rows,
        fetch_counts,
        hot_table,
        cold_table,
        ln_gain.reshape(1, -1),
        ln_bias.reshape(1, -1),
        w_in,
        w_out,
        out_grad,
    )
    return adagrad(cold_grad, hot_grad, cold_table, cold_accum, hot_table, hot_accum)


def solution(mesh):
    finer = Mesh(mesh.devices.reshape(NZ, NY, NC, NX), ALL)
    return jax.shard_map(
        on_device,
        mesh=finer,
        in_specs=(
            P(ALL, None),
            P(ALL, None),
            P(ALL, None),
            P(),
            P(),
            P(BY_ROWS, None),
            P(BY_ROWS),
            P(),
            P(),
            P(),
            P(),
            P(ALL, None),
        ),
        out_specs=(P(), P(), P(BY_ROWS, None), P(BY_ROWS)),
        check_vma=False,
    )
```

time: 201 us -> 101 us (0.50)
  Pallas kernels: 0 us -> 91.3 us
  blocking collectives: 68 us -> 0 us
  waiting for transfers between devices: 66.9 us -> 0 us
  starting transfers between devices: 24.8 us -> 0 us
  other arithmetic: 19 us -> 0 us
  matrix products: 7.64 us -> 0 us
  local copies, waits for them, and re-layouts: 12.9 us -> 8.88 us
    pallas_call x0 -> x2, Pallas kernels: none -> 91.3 us  [the longest x1 90.2 us: step(): pl.pallas_call(step_kernel, out_shape=(jax.ShapeDtypeStruct((NX, cold_row...]
    all_to_all x3 -> x0, blocking collectives: 68 us -> none  [the longest x1 29.7 us: on_device(): lax.all_to_all(wanted_rows, ROWS, split_axis=0, concat_axis=0, tiled=True)]
    all_to_all x5 -> x0, waiting for transfers between devices: 66.9 us -> none  [the longest x3 37.4 us: from_everyone(): lax.all_to_all(jnp.broadcast_to(value[None], (peers, *value.shape)), axis...]
    all_to_all x5 -> x0, starting transfers between devices: 24.8 us -> none  [the longest x3 13.4 us: from_everyone(): lax.all_to_all(jnp.broadcast_to(value[None], (peers, *value.shape)), axis...]
    dot_general x9 -> x0, matrix products: 7.64 us -> none  [the longest x2 3.73 us: hstu_layer(): jnp.dot(normed, w_in, preferred_element_type=jnp.float32)]
    unnamed x44 -> x24, local copies, waits for them, and re-layouts: 1.41 us -> 8.88 us
    reduce_sum x11 -> x0, other arithmetic: 6.03 us -> none  [the longest x1 1.87 us: over_copies(): return jnp.sum(everything, axis=0)]
    scatter-add x2 -> x0, other arithmetic: 4.19 us -> none  [the longest x1 2.21 us: on_device(): jax.ops.segment_sum(arrived.reshape(-1, feature_width), asked_rows.reshap...]
  transfers between devices with their start and end apart: 5 -> 0, of which waited for: 5 -> 0; matrix products, arithmetic and copies ran while one was open for 4% -> 0% of each run, Pallas kernels for 0% -> 0%
where the time goes in v1:
time: 101 us
  Pallas kernels  91.3 us (90%)
  local copies, waits for them, and re-layouts  8.88 us (9%)
    pallas_call x1, Pallas kernels, step(): pl.pallas_call(step_kernel, out_shape=(jax.ShapeDtypeStruct((NX, cold_row...  90.2 us
    unnamed x24, local copies, waits for them, and re-layouts  8.88 us

profile of v1, /device:TPU:1, one launch (start us, length us, event | category | flops | bytes accessed | tf_op | source)
XLA Modules:
  0.0 100.9 jit_solution(10450361107456683546)
XLA Ops:
  0.6 0.0 copy-start
  0.6 1.0 %copy-done = f32[256,512]{1,0:T(8,128)S(1)} copy-done((f32[256,512]{1,0:T(8,128)S(1)}, f32[256,512]{1,0:T(8,128)}, u32[]{:S(2)}) %copy-start) | copy-done | bytes 524312
  1.7 0.0 copy-start.1
  1.7 0.9 copy-done.1
  2.6 0.0 copy-start.4
  2.6 1.6 %copy-done.4 = bf16[512,2048]{1,0:T(8,128)(2,1)S(1)} copy-done((bf16[512,2048]{1,0:T(8,128)(2,1)S(1)}, bf16[512,2048]{1,0:T(8,128)(2,1)}, u32[]{:S(2)}) %copy-start.4) | copy-done | bytes 2097176
  4.2 0.0 copy-start.5
  4.2 1.0 %copy-done.5 = bf16[512,512]{1,0:T(8,128)(2,1)S(1)} copy-done((bf16[512,512]{1,0:T(8,128)(2,1)S(1)}, bf16[512,512]{1,0:T(8,128)(2,1)}, u32[]{:S(2)}) %copy-start.5) | copy-done | bytes 524312
  5.3 0.0 copy-start.6
  5.3 0.9 copy-done.6
  6.2 0.0 copy-start.7
  6.2 0.7 copy-done.7
  6.8 0.0 copy-start.8
  6.9 0.7 copy-done.8
  7.5 0.0 copy-start.9
  7.5 0.7 copy-done.9
  8.2 0.0 copy-start.10
  8.2 0.7 copy-done.10
  8.9 0.0 copy-start.11
  8.9 0.7 copy-done.11
  9.5 0.0 copy-start.2
  9.5 0.0 copy-start.3
  9.5 90.2 %step.1 = (f32[4,256,128]{2,1,0:T(8,128)S(1)}, f32[4,128,128]{2,1,0:T(8,128)S(1)}) custom-call(s32[1,128]{1,0:T(1,128)S(1)} %copy-done.10, s32[1,256]{1,0:T(1,128)S(1)} %copy-done.9, s32[1,128]{1,0:T(1,128)S(1)} %copy-done.11, f32[128,512]{1,0:T(8,128)S(1)} %copy-done.1, f32[256,512]{1,0:T(8,128)S(1)} %copy-done, f32[1,512]{1,0:T(1,128)S(1)} %bitcast.8, ...), custom_call_target="tpu_custom_call" | custom-call | flops 1500000000 | bytes 6000000 | tf_op jit(solution)/shard_map/step/pallas_call | solution.py:380
  99.7 0.0 copy-done.2
  99.8 0.0 copy-done.3
  99.8 1.1 %adagrad.1 = (f32[128,512]{1,0:T(8,128)}, f32[1,128]{1,0:T(1,128)}, f32[256,512]{1,0:T(8,128)}, f32[1,256]{1,0:T(1,128)}) custom-call(f32[4,256,128]{2,1,0:T(8,128)S(1)} %get-tuple-element.10.cold_ref, f32[4,128,128]{2,1,0:T(8,128)S(1)} %get-tuple-element.11.hot_ref, f32[256,512]{1,0:T(8,128)S(1)} %copy-done, f32[1,256]{1,0:T(1,128)S(1)} %bitcast.6, ...), custom_call_target="tpu_custom_call" | custom-call | tf_op jit(solution)/shard_map/adagrad/pallas_call | solution.py:455
Async XLA Ops:
  0.6 1.0 %copy-start = (f32[256,512]{1,0:T(8,128)S(1)}, f32[256,512]{1,0:T(8,128)}, u32[]{:S(2)}) copy-start(f32[256,512]{1,0:T(8,128)} %cold_table.1) | copy-start | bytes 1572868
  1.7 0.9 copy-start.1
  2.6 1.6 %copy-start.4 = (bf16[512,2048]{1,0:T(8,128)(2,1)S(1)}, bf16[512,2048]{1,0:T(8,128)(2,1)}, u32[]{:S(2)}) copy-start(bf16[512,2048]{1,0:T(8,128)(2,1)} %w_in_ref.1) | copy-start | bytes 6291460
  4.2 1.0 %copy-start.5 = (bf16[512,512]{1,0:T(8,128)(2,1)S(1)}, bf16[512,512]{1,0:T(8,128)(2,1)}, u32[]{:S(2)}) copy-start(bf16[512,512]{1,0:T(8,128)(2,1)} %w_out_ref.1) | copy-start | bytes 1572868
  5.3 0.9 copy-start.6
  6.2 0.7 copy-start.7
  6.8 0.7 copy-start.8
  7.5 0.7 copy-start.9
  8.2 0.7 copy-start.10
  8.9 0.7 copy-start.11
  9.5 90.2 %copy-start.2 = (f32[256]{0:T(256)S(1)}, f32[256]{0:T(256)}, u32[]{:S(2)}) copy-start(f32[256]{0:T(256)} %param.18) | copy-start | bytes 3076
  9.5 90.2 %copy-start.3 = (f32[128]{0:T(128)S(1)}, f32[128]{0:T(128)}, u32[]{:S(2)}) copy-start(f32[128]{0:T(128)} %param.16) | copy-start | bytes 1540

commit v2 on v1

--- a/solution.py
+++ b/solution.py
@@ -2,6 +2,7 @@
 
 import jax
 import jax.numpy as jnp
+import numpy as np
 from jax import lax
 from jax.experimental import pallas as pl
 from jax.experimental.pallas import tpu as pltpu
@@ -13,6 +14,24 @@
 NZ, NY, NC, NX = 8, 8, 2, 4
 NYC = NY * NC
 OWNERS = NZ * NYC
+INPUTS = 11
+GROUPS = 4
+SPAN = OWNERS // GROUPS
+
+
+def hops(offset, size):
+    return min(offset, size - offset)
+
+
+def farthest_first():
+    offsets = [(a, b, k) for a in range(NZ) for b in range(NY) for k in range(NC)]
+    mixed = [offsets[n * 37 % OWNERS] for n in range(OWNERS)]
+    far = lambda o: max(hops(o[0], NZ), hops(o[1], NY))
+    both = lambda o: hops(o[0], NZ) + hops(o[1], NY)
+    return sorted(mixed, key=lambda o: (-far(o), -both(o), o == (0, 0, 0)))
+
+
+OFFSETS = farthest_first()
 ALL = ("z", "y", "c", "x")
 BY_ROWS = ("z", "y", "c")
 MESH = pl.DeviceIdType.MESH
@@ -108,7 +127,14 @@
     )
 
 
-def step_kernel(
+def step_kernel(*refs):
+    sources, outputs = refs[:INPUTS], refs[INPUTS : INPUTS + 2]
+    held = refs[INPUTS + 2 : 2 * INPUTS + 2]
+    step_body(sources, *held, *outputs, *refs[2 * INPUTS + 2 :])
+
+
+def step_body(
+    sources,
     slots_ref,
     rows_ref,
     counts_ref,
@@ -119,8 +145,10 @@
     w_in_ref,
     w_out_ref,
     out_grad_ref,
+    offsets_ref,
     cold_out,
     hot_out,
+    load_sems,
     idx_z,
     idx_n,
     idx_all,
@@ -131,14 +159,15 @@
     x_recv,
     send_b,
     recv_b,
-    hot_c,
+    hot_s,
     hot_cr,
+    hot_xs,
+    hot_xr,
     hot_z,
     hot_zr,
     hot_t,
     hot_yr,
     hot_g,
-    hot_f,
     sems,
     z_s,
     z_r,
@@ -167,31 +196,34 @@
     width = hot_ref.shape[1]
     lanes = width // NX
 
-    def along(axis, o):
-        if axis == "z":
-            t = lax.rem(z + o, NZ)
-            return t, (t, y, c, x)
-        if axis == "y":
-            t = lax.rem(y + o, NY)
-            return t, (z, t, c, x)
+    def peers(axis):
         if axis == "yc":
-            t = lax.rem(yc + o, NYC)
-            return t, (z, lax.div(t, NC), lax.rem(t, NC), x)
-        t = lax.rem(x + o, NX)
-        return t, (z, y, c, t)
-
-    SIZE = {"z": NZ, "y": NY, "yc": NYC, "x": NX}
+            ways = [o[1:] for o in OFFSETS if o[0] == 0 and o != (0, 0, 0)]
+            for oy, oc in ways:
+                ty, tc = lax.rem(y + oy, NY), lax.rem(c + oc, NC)
+                yield ty * NC + tc, (z, ty, tc, x)
+            return
+        size = {"z": NZ, "y": NY, "x": NX}[axis]
+        for o in sorted(range(1, size), key=lambda o: -hops(o, size)):
+            if axis == "z":
+                t = lax.rem(z + o, NZ)
+                yield t, (t, y, c, x)
+            elif axis == "y":
+                t = lax.rem(y + o, NY)
+                yield t, (z, t, c, x)
+            else:
+                t = lax.rem(x + o, NX)
+                yield t, (z, y, c, t)
 
     def exchange(axis, src, dst, s, r):
         copies = []
-        for o in range(1, SIZE[axis]):
-            t, dev = along(axis, o)
+        for n, (t, dev) in enumerate(peers(axis)):
             copies.append(
                 pltpu.make_async_remote_copy(
                     src_ref=src(t),
                     dst_ref=dst,
-                    send_sem=s.at[o],
-                    recv_sem=r.at[o],
+                    send_sem=s.at[n],
+                    recv_sem=r.at[n],
                     device_id=dev,
                     device_id_type=MESH,
                 )
@@ -219,16 +251,12 @@
     def tile(q):
         return pl.ds(pl.multiple_of(q * 8, 8), 8)
 
-    def scatter_tiles(src, dst, n):
-        @pl.loop(1, OWNERS)
-        def _(o):
-            p = lax.rem(o * 37, OWNERS)
-            tz = lax.rem(z + lax.rem(p, NZ), NZ)
-            ty = lax.rem(y + lax.rem(lax.div(p, NZ), NY), NY)
-            tc = lax.rem(c + lax.div(p, NZ * NY), NC)
-            q = (ty * NC + tc) * NZ + tz
+    def scatter_tiles(src, dst, n, first, last, source):
+        for at in range(first, last):
+            oz, oy, oc = OFFSETS[at]
+            tz, ty, tc = lax.rem(z + oz, NZ), lax.rem(y + oy, NY), lax.rem(c + oc, NC)
             pltpu.make_async_remote_copy(
-                src_ref=src.at[tile(q)],
+                src_ref=src.at[tile(source(at, (ty * NC + tc) * NZ + tz))],
                 dst_ref=dst.at[tile(me)],
                 send_sem=sems.at[n],
                 recv_sem=sems.at[n + 1],
@@ -240,16 +268,37 @@
         whole = ref.at[pl.ds(0, (OWNERS - 1) * 8)]
         pltpu.make_async_copy(whole, whole, sems.at[n]).wait()
 
+    held = (
+        slots_ref,
+        rows_ref,
+        counts_ref,
+        hot_ref,
+        table_ref,
+        gain_ref,
+        bias_ref,
+        w_in_ref,
+        w_out_ref,
+        out_grad_ref,
+        offsets_ref,
+    )
+    loads = [
+        pltpu.make_async_copy(src, dst, load_sems.at[n])
+        for n, (src, dst) in enumerate(zip(sources, held))
+    ]
     barrier = pltpu.get_barrier_semaphore()
     greeted = 0
     for axis in ("z", "yc", "x"):
-        for o in range(1, SIZE[axis]):
-            pl.semaphore_signal(barrier, inc=1, device_id=along(axis, o)[1], device_id_type=MESH)
+        for _, dev in peers(axis):
+            pl.semaphore_signal(barrier, inc=1, device_id=dev, device_id_type=MESH)
             greeted += 1
+    for n in (1, 4, 0, 2, 3, 5, 6, 9, 10, 7, 8):
+        loads[n].start()
+    loads[1].wait()
     pl.semaphore_wait(barrier, greeted)
 
     pending = exchange("z", lambda t: rows_ref, idx_z.at[z], z_s, z_r)
     idx_z[z] = rows_ref[...]
+    loads[4].wait()
     table_high, table_low = two_parts(table_ref[...])
     arrived(pending)
     every = jnp.concatenate([idx_z[i] for i in range(NZ)], axis=0).astype(F32)
@@ -270,26 +319,37 @@
         found = dot(onehot, table_high) + dot(onehot, table_low)
         for i in range(NX):
             send_a[pl.ds(k * NX + i, OWNERS, stride=8), :] = found[:, i * lanes : (i + 1) * lanes]
-    scatter_tiles(send_a, recv_a, 0)
+    scatter_tiles(send_a, recv_a, 0, 0, OWNERS - 1, lambda at, q: q)
     recv_a[tile(me), :] = send_a[tile(me), :]
 
     both = jnp.where(lane == 0, columns[0], jnp.where(lane == 1, columns[1], 0.0))
     idx_n2 = jnp.transpose(both)[:8, :]
     idx_x[x] = idx_n2
-    more = exchange("x", lambda t: idx_x.at[x], idx_x.at[x], xi_s, xi_r)
-    pending += more
-
-    owner_of = lambda q: lax.rem(q, NZ) * NYC + lax.div(q, NZ)
+    idx_xs = exchange("x", lambda t: idx_x.at[x], idx_x.at[x], xi_s, xi_r)
+    pending += idx_xs
+
+    for n in (0, 2, 3, 5, 6, 9, 10, 7, 8):
+        loads[n].wait()
+    lane1 = iota((128, 128), 1)
+    row1 = iota((128, 128), 0)
     slot_of = jnp.transpose(jnp.broadcast_to(slots_ref[...].astype(F32), (128, 128)))
-    lane1 = iota((128, 128), 1)
-    order = (iota((128, 128), 0) == owner_of(lane1)).astype(BF16)
-    live = dot(jnp.broadcast_to(counts_ref[...].astype(F32), (8, 128)).astype(BF16), order)[:1, :]
+    counts = jnp.broadcast_to(counts_ref[...].astype(F32), (8, 128)).astype(BF16)
     hot_rows = hot_ref.shape[0]
+
+    def slot_picks(owner):
+        live = dot(counts, (row1 == owner).astype(BF16))[:1, :]
+        name = (hot_rows + 2 * owner).astype(F32)
+        return [((slot_of == name + k) & (live > k)).astype(BF16) for k in range(2)]
+
     pick_hot = (slot_of == lane1.astype(F32)).astype(BF16)
-    picks = []
-    for k in range(2):
-        name = (hot_rows + 2 * owner_of(lane1) + k).astype(F32)
-        picks.append(((slot_of == name) & (live > k)).astype(BF16))
+    picks = slot_picks(lax.rem(lane1, NZ) * NYC + lax.div(lane1, NZ))
+    off = offsets_ref[...]
+    ahead = (
+        lax.rem(z + off[0:1, :], NZ) * NYC
+        + lax.rem(y + off[1:2, :], NY) * NC
+        + lax.rem(c + off[2:3, :], NC)
+    )
+    back_picks = slot_picks(jnp.broadcast_to(ahead, (128, 128)))
     looked_hot = picked(pick_hot, hot_ref[...])
 
     tiles_wait(recv_a, 1)
@@ -306,72 +366,85 @@
     )
 
     high, low = two_parts(d_lookup)
-    for b, pick in enumerate([pick_hot] + picks):
-        total = dot(pick, high, ((0,), (0,))) + dot(pick, low, ((0,), (0,)))
+
+    def by_slot(pick):
+        return dot(pick, high, ((0,), (0,))) + dot(pick, low, ((0,), (0,)))
+
+    hot_s[...] = by_slot(pick_hot).reshape(2, 64, width)
+    swap = to_sibling(hot_s.at[1 - c], hot_cr, 4)
+    for k in range(2):
+        total = by_slot(back_picks[k])
         for i in range(NX):
-            x_send[i, b * 128 : (b + 1) * 128, :] = total[:, i * lanes : (i + 1) * lanes]
-    hot_part, cold_part = pl.ds(0, 128), pl.ds(128, 256)
-    hot_x = exchange("x", lambda t: x_send.at[t, hot_part], x_recv.at[x, hot_part], xh_s, xh_r)
-    cold_x = exchange("x", lambda t: x_send.at[t, cold_part], x_recv.at[x, cold_part], xc_s, xc_r)
-    pending += hot_x + cold_x
+            for g in range(GROUPS):
+                x_send[i, g, k] = total[g * SPAN : (g + 1) * SPAN, i * lanes : (i + 1) * lanes]
     x_recv[x] = x_send[x]
 
+    def start_cold(g):
+        return exchange("x", lambda t: x_send.at[t, g], x_recv.at[x, g], xc_s.at[g], xc_r.at[g])
+
+    cold_x = [start_cold(0)]
+    swap.wait()
+    for i in range(NX):
+        at = slice(i * lanes, (i + 1) * lanes)
+        hot_xs[i] = hot_s[c, :, at] + hot_cr[:, at]
+    hot_x = exchange("x", lambda t: hot_xs.at[t], hot_xr.at[x], xh_s, xh_r)
+    hot_xr[x] = hot_xs[x]
+    cold_x += [start_cold(g) for g in range(1, GROUPS)]
+
+    def send_group(g):
+        arrived(cold_x[g])
+        for p in range(NX):
+            for k in range(2):
+                send_b[pl.ds(g * SPAN * 8 + p * 2 + k, SPAN, stride=8), :] = x_recv[p, g, k]
+        last = min((g + 1) * SPAN, OWNERS - 1)
+        scatter_tiles(send_b, recv_b, 2, g * SPAN, last, lambda at, q: at)
+        return cold_x[g]
+
+    pending += hot_x
+    pending += send_group(0)
+    pending += send_group(1)
     arrived(hot_x)
-    hot = x_recv[0, :128] + x_recv[1, :128] + x_recv[2, :128] + x_recv[3, :128]
-    hot_c[...] = hot.reshape(2, 64, 128)
-    swap = to_sibling(hot_c.at[1 - c], hot_cr, 4)
-    arrived(cold_x)
-    for p in range(NX):
-        for k in range(2):
-            send_b[pl.ds(p * 2 + k, OWNERS, stride=8), :] = x_recv[
-                p, 128 + k * 128 : 256 + k * 128, :
-            ]
-    swap.wait()
-    hot_z[...] = (hot_c[c] + hot_cr[...]).reshape(NZ, 8, 128)
+    hot_z[...] = (hot_xr[0] + hot_xr[1] + hot_xr[2] + hot_xr[3]).reshape(NZ, 8, 128)
     hot_zs = exchange("z", lambda t: hot_z.at[t], hot_zr.at[z], hz_s, hz_r)
     hot_zr[z] = hot_z[z]
-    pending += hot_zs
-    scatter_tiles(send_b, recv_b, 2)
-    recv_b[tile(me), :] = send_b[tile(me), :]
+    pending += send_group(2)
+    pending += send_group(3)
+    recv_b[tile(me), :] = send_b[tile(OWNERS - 1), :]
+
+    arrived(idx_xs)
+    tall = iota((table_ref.shape[0], OWNERS), 0).astype(F32)
+    sums = [(tall == idx_x[p, k : k + 1, :]).astype(BF16) for p in range(NX) for k in range(2)]
+
     arrived(hot_zs)
     hot_t[0] = jnp.sum(hot_zr[...], axis=0)
     hot_ys = exchange("y", lambda t: hot_t.at[0], hot_yr.at[y], hy_s, hy_r)
     hot_yr[y] = hot_t[0]
-    pending += hot_ys
     arrived(hot_ys)
     hot_t[1] = jnp.sum(hot_yr[...], axis=0)
     hot_gs = exchange("z", lambda t: hot_t.at[1], hot_g.at[z], hg_s, hg_r)
     hot_g[z] = hot_t[1]
-    pending += hot_gs
-    arrived(hot_gs)
-    hot_f[c] = hot_g[...].reshape(64, 128)
-    swap = to_sibling(hot_f.at[c], hot_f.at[c], 6)
-    swap.wait()
-    hot_out[x] = hot_f[...].reshape(128, 128)
-    hot_os = exchange("x", lambda t: hot_out.at[x], hot_out.at[x], xo_s, xo_r)
-    pending += hot_os
-
-    arrived(pending[2 * 0 + (NZ - 1) + (NYC - 1) : (NZ - 1) + (NYC - 1) + (NX - 1)])
-    tall = iota((table_ref.shape[0], OWNERS), 0).astype(F32)
-    sums = [
-        (tall == idx_x[p, k : k + 1, :]).astype(BF16) for p in range(NX) for k in range(2)
-    ]
+
     tiles_wait(recv_b, 3)
     grad = jnp.zeros((table_ref.shape[0], 128), F32)
     for n in range(8):
         grad = grad + picked(sums[n], recv_b[pl.ds(n, OWNERS, stride=8), :])
     cold_out[x] = grad
     cold_os = exchange("x", lambda t: cold_out.at[x], cold_out.at[x], xp_s, xp_r)
-    pending += cold_os
+    arrived(hot_gs)
+    hot_out[c, x] = hot_g[...].reshape(64, 128)
+    hot_os = exchange("x", lambda t: hot_out.at[c, x], hot_out.at[c, x], xo_s, xo_r)
     arrived(hot_os)
+    swap = to_sibling(hot_out.at[c], hot_out.at[c], 6)
     arrived(cold_os)
-    for cp in pending:
+    swap.wait()
+    for cp in pending + hot_zs + hot_ys + hot_gs + cold_os + hot_os:
         cp.wait_send()
     tiles_wait(recv_a, 0)
     tiles_wait(recv_b, 2)
 
 
-def step(slots, rows, counts, hot_table, cold_table, gain, bias, w_in, w_out, out_grad):
+def step(*args):
+    hot_table, cold_table = args[3:5]
     vm = pl.BlockSpec(memory_space=pltpu.VMEM)
     dma = pltpu.SemaphoreType.DMA
     cold_rows, width = cold_table.shape
@@ -381,35 +454,39 @@
         step_kernel,
         out_shape=(
             jax.ShapeDtypeStruct((NX, cold_rows, width // NX), F32),
-            jax.ShapeDtypeStruct((NX, hot_table.shape[0], width // NX), F32),
+            jax.ShapeDtypeStruct((NC, NX, hot_table.shape[0] // NC, width // NX), F32),
         ),
-        in_specs=[vm] * 10,
+        in_specs=[pl.BlockSpec(memory_space=pltpu.HBM)] * INPUTS,
         out_specs=(vm, vm),
         scratch_shapes=[
+            *[pltpu.VMEM(a.shape, a.dtype) for a in args],
+            dma((INPUTS,)),
             pltpu.VMEM((NZ, 1, 256), jnp.int32),
             f32(8, 128),
             f32(NYC, 8, 128),
             f32(NX, 8, 128),
             f32(OWNERS * 8, 128),
             f32(OWNERS * 8, 128),
-            f32(NX, 384, 128),
-            f32(NX, 384, 128),
+            f32(NX, GROUPS, 2, SPAN, 128),
+            f32(NX, GROUPS, 2, SPAN, 128),
             f32(OWNERS * 8, 128),
             f32(OWNERS * 8, 128),
-            f32(2, 64, 128),
-            f32(64, 128),
+            f32(2, 64, width),
+            f32(64, width),
+            f32(NX, 64, 128),
+            f32(NX, 64, 128),
             f32(NZ, 8, 128),
             f32(NZ, 8, 128),
             f32(2, 8, 128),
             f32(NY, 8, 128),
             f32(NZ, 8, 128),
-            f32(2, 64, 128),
             dma((8,)),
             *two(NZ),
             *two(NYC),
             *two(NX),
             *two(NX),
-            *two(NX),
+            dma((GROUPS, NX)),
+            dma((GROUPS, NX)),
             *two(NZ),
             *two(NY),
             *two(NZ),
@@ -417,36 +494,38 @@
             *two(NX),
         ],
         compiler_params=pltpu.CompilerParams(
-            collective_id=0, has_side_effects=True, vmem_limit_bytes=48 << 20
+            collective_id=0, has_side_effects=True, vmem_limit_bytes=61 << 20
         ),
         cost_estimate=pl.CostEstimate(
             flops=1_500_000_000, bytes_accessed=6_000_000, transcendentals=400_000
         ),
         name="step",
-    )(slots, rows, counts, hot_table, cold_table, gain, bias, w_in, w_out, out_grad)
-
-
-def update(grad_ref, table_ref, accum_ref, new_table, new_accum):
-    rows = table_ref.shape[0]
-    lanes = grad_ref.shape[2]
-    total = sum(grad_ref[i] * grad_ref[i] for i in range(NX))
-    mean = jnp.sum(total, axis=1, keepdims=True) * (1.0 / table_ref.shape[1])
+    )(*args)
+
+
+def update(blocks, table_ref, accum_ref, new_table, new_accum):
+    rows, width = table_ref.shape
+    lanes = width // NX
     for b in range(rows // 128):
         at = slice(b * 128, (b + 1) * 128)
+        grads = blocks(b)
+        mean = jnp.sum(sum(g * g for g in grads), axis=1, keepdims=True) * (1.0 / width)
         old = jnp.transpose(jnp.broadcast_to(accum_ref[:, at], (128, 128)))
-        new = old + mean[at, :]
+        new = old + mean
         new_accum[:, at] = jnp.transpose(new)[:1, :]
         rate = STEP_RATE * lax.rsqrt(new)
         for i in range(NX):
             col = slice(i * lanes, (i + 1) * lanes)
-            new_table[at, col] = table_ref[at, col] - grad_ref[i, at, :] * rate
+            new_table[at, col] = table_ref[at, col] - grads[i] * rate
 
 
 def adagrad_kernel(
     cold_ref, hot_ref, cold_table, cold_accum, hot_table, hot_accum, o_hot, o_hacc, o_cold, o_cacc
 ):
-    update(hot_ref, hot_table, hot_accum, o_hot, o_hacc)
-    update(cold_ref, cold_table, cold_accum, o_cold, o_cacc)
+    halves = lambda i: jnp.concatenate([hot_ref[0, i], hot_ref[1, i]], axis=0)
+    update(lambda b: [halves(i) for i in range(NX)], hot_table, hot_accum, o_hot, o_hacc)
+    cold = lambda b: [cold_ref[i, b * 128 : (b + 1) * 128, :] for i in range(NX)]
+    update(cold, cold_table, cold_accum, o_cold, o_cacc)
 
 
 def adagrad(cold_grad, hot_grad, cold_table, cold_accum, hot_table, hot_accum):
@@ -491,6 +570,7 @@
         w_in,
         w_out,
         out_grad,
+        jnp.asarray(np.array(OFFSETS, np.int32).T),
     )
     return adagrad(cold_grad, hot_grad, cold_table, cold_accum, hot_table, hot_accum)
 

time: 101 us -> 83.5 us (0.83)
  Pallas kernels: 91.3 us -> 80.6 us
  local copies, waits for them, and re-layouts: 8.88 us -> 2 us
    pallas_call x1, Pallas kernels: 90.2 us -> 79.5 us  [step(): pl.pallas_call(step_kernel, out_shape=(jax.ShapeDtypeStruct((NX, cold_row...]
    unnamed x24 -> x12, local copies, waits for them, and re-layouts: 8.88 us -> 2 us
where the time goes in v2:
time: 83.5 us; the launch traced here: 83.3 us
  Pallas kernels  80.6 us (97%)
  local copies, waits for them, and re-layouts  2 us (2%)
    pallas_call x1, Pallas kernels, step(): pl.pallas_call(step_kernel, out_shape=(jax.ShapeDtypeStruct((NX, cold_row...  79.5 us
    unnamed x12, local copies, waits for them, and re-layouts  2 us

profile of v2, /device:TPU:1, one launch (start us, length us, event | category | flops | bytes accessed | tf_op | source)
XLA Modules:
  0.0 83.3 jit_solution(7116489202790793275)
XLA Ops:
  0.6 0.0 copy-start
  0.6 0.0 copy-start.2
  0.7 0.0 copy-start.4
  0.7 0.0 copy-start.5
  0.7 79.5 %step.1 = (f32[4,256,128]{2,1,0:T(8,128)}, f32[2,4,64,128]{3,2,1,0:T(8,128)}) custom-call(s32[1,128]{1,0:T(1,128)} %refs_0_.1, s32[1,256]{1,0:T(1,128)} %refs_1_.1, s32[1,128]{1,0:T(1,128)} %refs_2_.1, f32[128,512]{1,0:T(8,128)} %hot_table.1, f32[256,512]{1,0:T(8,128)} %cold_table.1, f32[1,512]{1,0:T(1,128)} %bitcast.8, f32[1,512]{1,0:T(1,128)} %bitcast.9, ...), custom_call_target="tpu_custom_call" | custom-call | flops 1500000000 | bytes 6000000 | tf_op jit(solution)/shard_map/step/pallas_call | solution.py:453
  80.2 0.0 copy-done
  80.2 0.0 copy-done.2
  80.2 0.0 copy-done.4
  80.2 0.0 copy-done.5
  80.2 0.0 copy-start.1
  80.2 1.0 %copy-done.1 = f32[4,256,128]{2,1,0:T(8,128)S(1)} copy-done((f32[4,256,128]{2,1,0:T(8,128)S(1)}, f32[4,256,128]{2,1,0:T(8,128)}, u32[]{:S(2)}) %copy-start.1) | copy-done | bytes 524312
  81.3 0.0 copy-start.3
  81.3 0.9 %copy-done.3 = f32[2,4,64,128]{3,2,1,0:T(8,128)S(1)} copy-done((f32[2,4,64,128]{3,2,1,0:T(8,128)S(1)}, f32[2,4,64,128]{3,2,1,0:T(8,128)}, u32[]{:S(2)}) %copy-start.3) | copy-done | bytes 262168
  82.2 1.1 %adagrad.1 = (f32[128,512]{1,0:T(8,128)}, f32[1,128]{1,0:T(1,128)}, f32[256,512]{1,0:T(8,128)}, f32[1,256]{1,0:T(1,128)}) custom-call(f32[4,256,128]{2,1,0:T(8,128)S(1)} %copy-done.1, f32[2,4,64,128]{3,2,1,0:T(8,128)S(1)} %copy-done.3, f32[256,512]{1,0:T(8,128)S(1)} %copy-done, f32[1,256]{1,0:T(1,128)S(1)} %bitcast.6, f32[128,512]{1,0:T(8,128)S(1)} %copy-done.2, ...), custom_call_target="tpu_custom_call" | custom-call | tf_op jit(solution)/shard_map/adagrad/pallas_call | solution.py:534
Async XLA Ops:
  0.6 79.6 %copy-start = (f32[256,512]{1,0:T(8,128)S(1)}, f32[256,512]{1,0:T(8,128)}, u32[]{:S(2)}) copy-start(f32[256,512]{1,0:T(8,128)} %cold_table.1) | copy-start | bytes 1572868
  0.6 79.6 %copy-start.2 = (f32[128,512]{1,0:T(8,128)S(1)}, f32[128,512]{1,0:T(8,128)}, u32[]{:S(2)}) copy-start(f32[128,512]{1,0:T(8,128)} %hot_table.1) | copy-start | bytes 786436
  0.7 79.6 %copy-start.4 = (f32[256]{0:T(256)S(1)}, f32[256]{0:T(256)}, u32[]{:S(2)}) copy-start(f32[256]{0:T(256)} %param.19) | copy-start | bytes 3076
  0.7 79.6 %copy-start.5 = (f32[128]{0:T(128)S(1)}, f32[128]{0:T(128)}, u32[]{:S(2)}) copy-start(f32[128]{0:T(128)} %param.17) | copy-start | bytes 1540
  80.2 1.0 %copy-start.1 = (f32[4,256,128]{2,1,0:T(8,128)S(1)}, f32[4,256,128]{2,1,0:T(8,128)}, u32[]{:S(2)}) copy-start(f32[4,256,128]{2,1,0:T(8,128)} %get-tuple-element.10.cold_ref) | copy-start | bytes 1572868
  81.3 0.9 %copy-start.3 = (f32[2,4,64,128]{3,2,1,0:T(8,128)S(1)}, f32[2,4,64,128]{3,2,1,0:T(8,128)}, u32[]{:S(2)}) copy-start(f32[2,4,64,128]{3,2,1,0:T(8,128)} %get-tuple-element.11.hot_ref) | copy-start | bytes 786436

commit v3 on v2

--- a/solution.py
+++ b/solution.py
@@ -61,9 +61,9 @@
     return lax.broadcasted_iota(jnp.int32, shape, dim)
 
 
-def layer_gradient(looked_up, gain, bias, w_in_ref, w_out_ref, out_grad):
+def layer_gradient(looked_up, gain, bias, w_in_ref, d_gated, out_grad):
     seq, width = looked_up.shape
-    inner = w_out_ref.shape[0]
+    inner = d_gated.shape[1]
     mean = jnp.mean(looked_up, axis=1, keepdims=True)
     centered = looked_up - mean
     inv = lax.rsqrt(jnp.mean(centered * centered, axis=1, keepdims=True) + 1e-05)
@@ -93,7 +93,6 @@
     mixed = mixed - jnp.mean(mixed, axis=1, keepdims=True)
     inv2 = lax.rsqrt(jnp.mean(mixed * mixed, axis=1, keepdims=True) + 1e-06)
     mhat = mixed * inv2
-    d_gated = dot(out_grad, w_out_ref[...], ((1,), (1,))).astype(BF16).astype(F32)
     d_gates = (d_gated * mhat).astype(BF16)
     d_mhat = d_gated * gates.astype(F32)
     d_mixed = inv2 * (
@@ -161,13 +160,11 @@
     recv_b,
     hot_s,
     hot_cr,
-    hot_xs,
-    hot_xr,
     hot_z,
     hot_zr,
     hot_t,
     hot_yr,
-    hot_g,
+    hot_t2,
     sems,
     z_s,
     z_r,
@@ -175,8 +172,6 @@
     yc_r,
     xi_s,
     xi_r,
-    xh_s,
-    xh_r,
     xc_s,
     xc_r,
     hz_s,
@@ -185,8 +180,6 @@
     hy_r,
     hg_s,
     hg_r,
-    xo_s,
-    xo_r,
     xp_s,
     xp_r,
 ):
@@ -202,6 +195,12 @@
             for oy, oc in ways:
                 ty, tc = lax.rem(y + oy, NY), lax.rem(c + oc, NC)
                 yield ty * NC + tc, (z, ty, tc, x)
+            return
+        if axis == "zx":
+            ways = [(a, b) for a in range(NZ) for b in range(NX) if (a, b) != (0, 0)]
+            for oz, ox in sorted(ways, key=lambda o: -hops(o[0], NZ) - hops(o[1], NX)):
+                tz, tx = lax.rem(z + oz, NZ), lax.rem(x + ox, NX)
+                yield (tz, tx), (tz, y, c, tx)
             return
         size = {"z": NZ, "y": NY, "x": NX}[axis]
         for o in sorted(range(1, size), key=lambda o: -hops(o, size)):
@@ -351,7 +350,9 @@
     )
     back_picks = slot_picks(jnp.broadcast_to(ahead, (128, 128)))
     looked_hot = picked(pick_hot, hot_ref[...])
-
+    d_gated = dot(out_grad_ref[...], w_out_ref[...], ((1,), (1,))).astype(BF16).astype(F32)
+
+    arrived(idx_xs)
     tiles_wait(recv_a, 1)
     looked = []
     for i in range(NX):
@@ -362,7 +363,7 @@
     looked_up = jnp.concatenate(looked, axis=1)
 
     d_lookup = layer_gradient(
-        looked_up, gain_ref[...], bias_ref[...], w_in_ref, w_out_ref, out_grad_ref[...]
+        looked_up, gain_ref[...], bias_ref[...], w_in_ref, d_gated, out_grad_ref[...]
     )
 
     high, low = two_parts(d_lookup)
@@ -384,11 +385,11 @@
 
     cold_x = [start_cold(0)]
     swap.wait()
+    own = (hot_s[c] + hot_cr[...]).reshape(NZ, 8, width)
     for i in range(NX):
-        at = slice(i * lanes, (i + 1) * lanes)
-        hot_xs[i] = hot_s[c, :, at] + hot_cr[:, at]
-    hot_x = exchange("x", lambda t: hot_xs.at[t], hot_xr.at[x], xh_s, xh_r)
-    hot_xr[x] = hot_xs[x]
+        hot_z[:, i] = own[:, :, i * lanes : (i + 1) * lanes]
+    hot_zs = exchange("zx", lambda t: hot_z.at[t[0], t[1]], hot_zr.at[z, x], hz_s, hz_r)
+    hot_zr[z, x] = hot_z[z, x]
     cold_x += [start_cold(g) for g in range(1, GROUPS)]
 
     def send_group(g):
@@ -400,29 +401,23 @@
         scatter_tiles(send_b, recv_b, 2, g * SPAN, last, lambda at, q: at)
         return cold_x[g]
 
-    pending += hot_x
     pending += send_group(0)
     pending += send_group(1)
-    arrived(hot_x)
-    hot_z[...] = (hot_xr[0] + hot_xr[1] + hot_xr[2] + hot_xr[3]).reshape(NZ, 8, 128)
-    hot_zs = exchange("z", lambda t: hot_z.at[t], hot_zr.at[z], hz_s, hz_r)
-    hot_zr[z] = hot_z[z]
     pending += send_group(2)
+    arrived(hot_zs)
+    hot_t[...] = jnp.sum(hot_zr[...].reshape(NZ * NX, 8, 128), axis=0)
+    hot_ys = exchange("y", lambda t: hot_t, hot_yr.at[y], hy_s, hy_r)
+    hot_yr[y] = hot_t[...]
     pending += send_group(3)
     recv_b[tile(me), :] = send_b[tile(OWNERS - 1), :]
 
-    arrived(idx_xs)
     tall = iota((table_ref.shape[0], OWNERS), 0).astype(F32)
     sums = [(tall == idx_x[p, k : k + 1, :]).astype(BF16) for p in range(NX) for k in range(2)]
 
-    arrived(hot_zs)
-    hot_t[0] = jnp.sum(hot_zr[...], axis=0)
-    hot_ys = exchange("y", lambda t: hot_t.at[0], hot_yr.at[y], hy_s, hy_r)
-    hot_yr[y] = hot_t[0]
     arrived(hot_ys)
-    hot_t[1] = jnp.sum(hot_yr[...], axis=0)
-    hot_gs = exchange("z", lambda t: hot_t.at[1], hot_g.at[z], hg_s, hg_r)
-    hot_g[z] = hot_t[1]
+    hot_t2[...] = jnp.sum(hot_yr[...], axis=0)
+    hot_gs = exchange("zx", lambda t: hot_t2, hot_out.at[c, z, x], hg_s, hg_r)
+    hot_out[c, z, x] = hot_t2[...]
 
     tiles_wait(recv_b, 3)
     grad = jnp.zeros((table_ref.shape[0], 128), F32)
@@ -431,13 +426,10 @@
     cold_out[x] = grad
     cold_os = exchange("x", lambda t: cold_out.at[x], cold_out.at[x], xp_s, xp_r)
     arrived(hot_gs)
-    hot_out[c, x] = hot_g[...].reshape(64, 128)
-    hot_os = exchange("x", lambda t: hot_out.at[c, x], hot_out.at[c, x], xo_s, xo_r)
-    arrived(hot_os)
     swap = to_sibling(hot_out.at[c], hot_out.at[c], 6)
     arrived(cold_os)
     swap.wait()
-    for cp in pending + hot_zs + hot_ys + hot_gs + cold_os + hot_os:
+    for cp in pending + hot_zs + hot_ys + hot_gs + cold_os:
         cp.wait_send()
     tiles_wait(recv_a, 0)
     tiles_wait(recv_b, 2)
@@ -453,8 +445,8 @@
     return pl.pallas_call(
         step_kernel,
         out_shape=(
-            jax.ShapeDtypeStruct((NX, cold_rows, width // NX), F32),
-            jax.ShapeDtypeStruct((NC, NX, hot_table.shape[0] // NC, width // NX), F32),
+            pltpu.VMEM((NX, cold_rows, width // NX), F32),
+            pltpu.VMEM((NC, NZ, NX, hot_table.shape[0] // (NC * NZ), width // NX), F32),
         ),
         in_specs=[pl.BlockSpec(memory_space=pltpu.HBM)] * INPUTS,
         out_specs=(vm, vm),
@@ -473,24 +465,20 @@
             f32(OWNERS * 8, 128),
             f32(2, 64, width),
             f32(64, width),
-            f32(NX, 64, 128),
-            f32(NX, 64, 128),
-            f32(NZ, 8, 128),
-            f32(NZ, 8, 128),
-            f32(2, 8, 128),
+            f32(NZ, NX, 8, 128),
+            f32(NZ, NX, 8, 128),
+            f32(8, 128),
             f32(NY, 8, 128),
-            f32(NZ, 8, 128),
+            f32(8, 128),
             dma((8,)),
             *two(NZ),
             *two(NYC),
             *two(NX),
-            *two(NX),
             dma((GROUPS, NX)),
             dma((GROUPS, NX)),
-            *two(NZ),
+            *two(NZ * NX),
             *two(NY),
-            *two(NZ),
-            *two(NX),
+            *two(NZ * NX),
             *two(NX),
         ],
         compiler_params=pltpu.CompilerParams(
@@ -522,8 +510,8 @@
 def adagrad_kernel(
     cold_ref, hot_ref, cold_table, cold_accum, hot_table, hot_accum, o_hot, o_hacc, o_cold, o_cacc
 ):
-    halves = lambda i: jnp.concatenate([hot_ref[0, i], hot_ref[1, i]], axis=0)
-    update(lambda b: [halves(i) for i in range(NX)], hot_table, hot_accum, o_hot, o_hacc)
+    hot = lambda i: hot_ref[:, :, i].reshape(128, 128)
+    update(lambda b: [hot(i) for i in range(NX)], hot_table, hot_accum, o_hot, o_hacc)
     cold = lambda b: [cold_ref[i, b * 128 : (b + 1) * 128, :] for i in range(NX)]
     update(cold, cold_table, cold_accum, o_cold, o_cacc)
 

time: 83.5 us -> 75.9 us (0.909)
  Pallas kernels: 80.6 us -> 75.1 us
  local copies, waits for them, and re-layouts: 2 us -> 0.02 us
    pallas_call x1, Pallas kernels: 79.5 us -> 74 us  [step(): pl.pallas_call(step_kernel, out_shape=(pltpu.VMEM((NX, cold_rows, width /...]
    unnamed x12 -> x8, local copies, waits for them, and re-layouts: 2 us -> 0.02 us
where the time goes in v3:
time: 75.9 us; the launch traced here: 75.8 us
  Pallas kernels  75.1 us (99%)
    pallas_call x1, Pallas kernels, step(): pl.pallas_call(step_kernel, out_shape=(pltpu.VMEM((NX, cold_rows, width /...  74 us

profile of v3, /device:TPU:1, one launch (start us, length us, event | category | flops | bytes accessed | tf_op | source)
XLA Modules:
  0.0 75.8 jit_solution(1402307003968677574)
XLA Ops:
  0.6 0.0 copy-start
  0.6 0.0 copy-start.1
  0.7 0.0 copy-start.2
  0.7 0.0 copy-start.3
  0.7 74.0 %step.1 = (f32[4,256,128]{2,1,0:T(8,128)S(1)}, f32[2,8,4,8,128]{4,3,2,1,0:T(8,128)S(1)}) custom-call(s32[1,128]{1,0:T(1,128)} %refs_0_.1, s32[1,256]{1,0:T(1,128)} %refs_1_.1, s32[1,128]{1,0:T(1,128)} %refs_2_.1, f32[128,512]{1,0:T(8,128)} %hot_table.1, f32[256,512]{1,0:T(8,128)} %cold_table.1, f32[1,512]{1,0:T(1,128)} %bitcast.8, f32[1,512]{1,0:T(1,128)} %bitcast.9, ...), custom_call_target="tpu_custom_call" | custom-call | flops 1500000000 | bytes 6000000 | tf_op jit(solution)/shard_map/step/pallas_call | solution.py:445
  74.7 0.0 copy-done
  74.7 0.0 copy-done.1
  74.7 0.0 copy-done.2
  74.7 0.0 copy-done.3
  74.7 1.1 %adagrad.1 = (f32[128,512]{1,0:T(8,128)}, f32[1,128]{1,0:T(1,128)}, f32[256,512]{1,0:T(8,128)}, f32[1,256]{1,0:T(1,128)}) custom-call(f32[4,256,128]{2,1,0:T(8,128)S(1)} %get-tuple-element.10.cold_ref, f32[2,8,4,8,128]{4,3,2,1,0:T(8,128)S(1)} %get-tuple-element.11.hot_ref, f32[256,512]{1,0:T(8,128)S(1)} %copy-done, f32[1,256]{1,0:T(1,128)S(1)} %bitcast.6, ...), custom_call_target="tpu_custom_call" | custom-call | tf_op jit(solution)/shard_map/adagrad/pallas_call | solution.py:522
Async XLA Ops:
  0.6 74.0 %copy-start = (f32[256,512]{1,0:T(8,128)S(1)}, f32[256,512]{1,0:T(8,128)}, u32[]{:S(2)}) copy-start(f32[256,512]{1,0:T(8,128)} %cold_table.1) | copy-start | bytes 1572868
  0.6 74.0 %copy-start.1 = (f32[128,512]{1,0:T(8,128)S(1)}, f32[128,512]{1,0:T(8,128)}, u32[]{:S(2)}) copy-start(f32[128,512]{1,0:T(8,128)} %hot_table.1) | copy-start | bytes 786436
  0.7 74.0 %copy-start.2 = (f32[256]{0:T(256)S(1)}, f32[256]{0:T(256)}, u32[]{:S(2)}) copy-start(f32[256]{0:T(256)} %param.19) | copy-start | bytes 3076
  0.7 74.0 %copy-start.3 = (f32[128]{0:T(128)S(1)}, f32[128]{0:T(128)}, u32[]{:S(2)}) copy-start(f32[128]{0:T(128)} %param.17) | copy-start | bytes 1540
